TPU v7x, 256 devices: a whole 4x4x8 slice. The times are simulated.
256 devices in a mesh: tower: 2 (over x_lo), seq: 16 (over z, core), head: 8 (over x_hi, y).
Axes of the slice: x: 4 (x_hi: 2, x_lo: 2; x = x_hi * 2 + x_lo), y: 4, z: 8, core: 2. Of those that a mesh axis runs over, the one named last changes fastest.
Arguments:
- acts: bfloat16 [2, 8192, 5, 3072], P('tower', ('seq', 'head')), may hold values from -36 to 36, as said below
- out_weight: bfloat16 [2, 3072, 3072], P('tower', 'head'), may hold values from -0.109375 to 0.109375
- pairs: int32 [2, 32, 3], P('tower', 'seq'), may hold values from -1 to 31, as said below
Outputs:
- mixed: bfloat16 [2, 8192, 3072], P('tower', ('seq', 'head'))
Inputs may be any that keep to these rules, and one draw needn't show every extreme that they name: `pairs`: slot k of block i holds i - 1 + k or -1; slot 1 always holds i; block i of one tower lists j exactly where block j of the other tower lists i; some block of each tower has all three slots filled. `acts`: finite values.
All inputs are finite; a program needn't handle non-finite values.
Results may differ from a plain program's by a relative error of at most 0.018.
Values may be sent and summed in bfloat16 or wider, within the bound.
A program may use at most 128 MiB of HBM per device.

v0:
```python
import math

import jax
import jax.numpy as jnp
from jax import lax
from jax.sharding import PartitionSpec as P

DH = 128


def from_partner(value, axis, bit):
    mask = 2**bit
    pairs = [(source, source ^ mask) for source in range(lax.axis_size(axis))]
    return lax.ppermute(value, axis, pairs)


def from_behind(shard, axis, by):
    devices = lax.axis_size(axis)
    pairs = [(i, i + by) for i in range(devices) if 0 <= i + by < devices]
    return lax.ppermute(shard, axis, pairs)


def attend_piece(carry, queries, piece, key_blocks, query_ids):
    count = piece.shape[0]
    step_rows = math.gcd(count, 512)
    heads_dev = queries.shape[1]
    tiles = piece.reshape(count // step_rows, step_rows, 2, heads_dev, DH)
    if key_blocks is None:
        tile_ids = jnp.zeros((count // step_rows, step_rows), jnp.int32)
    else:
        tile_ids = key_blocks.reshape(count // step_rows, step_rows)

    def advance(state, inputs):
        peak, total, accum = state
        tile, block_ids = inputs
        scores = jnp.einsum(
            "qhd,khd->hqk", queries, tile[:, 0], preferred_element_type=jnp.float32
        ) * DH ** (-0.5)
        if query_ids is not None:
            allowed = jnp.any(
                (query_ids[:, :, None] == block_ids[None, None, :]) & (query_ids[:, :, None] >= 0),
                axis=1,
            )
            scores = jnp.where(allowed[None], scores, -1e30)
        fresh = jnp.maximum(peak, jnp.max(scores, axis=2))
        weights = jnp.exp(scores - fresh[:, :, None])
        if query_ids is not None:
            weights = jnp.where(allowed[None], weights, 0.0)
        shrink = jnp.exp(peak - fresh)
        total = total * shrink + jnp.sum(weights, axis=2)
        update = jnp.einsum(
            "hqk,khd->qhd",
            weights.astype(jnp.bfloat16),
            tile[:, 1],
            preferred_element_type=jnp.float32,
        )
        accum = accum * shrink.T[:, :, None] + update
        return ((fresh, total, accum), None)

    result, unused = lax.scan(advance, carry, (tiles, tile_ids))
    return result


def finish(carry):
    peak, total, accum = carry
    return accum / total.T[:, :, None]


def on_device(acts, out_weight, pairs):
    local = acts[0]
    model_width = local.shape[2]
    other = from_partner(local[:, 3:5], "tower", 0)
    mine, theirs = (
        lax.all_to_all(local[:, 0:3], "head", split_axis=2, concat_axis=0, tiled=True),
        lax.all_to_all(other, "head", split_axis=2, concat_axis=0, tiled=True),
    )
    rows = mine.shape[0]
    width = mine.shape[2]
    heads_dev = width // DH
    blocks_here = pairs.shape[1]
    block_rows = rows // blocks_here
    queries = mine[:, 0].reshape(rows, heads_dev, DH)
    self_pairs = mine[:, 1:3]
    start_carry = (
        jnp.full((heads_dev, rows), -1e30, jnp.float32),
        jnp.zeros((heads_dev, rows), jnp.float32),
        jnp.zeros((rows, heads_dev, DH), jnp.float32),
    )
    self_out = finish(
        attend_piece(
            start_carry, queries, lax.all_gather(self_pairs, "seq", axis=0, tiled=True), None, None
        )
    )
    query_ids = jnp.repeat(pairs[0], block_rows, axis=0)
    first_block = lax.axis_index("seq") * blocks_here
    before = from_behind(theirs, "seq", 1)
    behind = from_behind(theirs, "seq", -1)
    joined = jnp.concatenate([before, theirs, behind], axis=0)
    key_blocks = (
        first_block - blocks_here + jnp.arange(joined.shape[0], dtype=jnp.int32) // block_rows
    )
    cross_carry = attend_piece(start_carry, queries, joined, key_blocks, query_ids)
    cross_out = finish(cross_carry)
    attn = (self_out + cross_out).reshape(rows, width).astype(jnp.bfloat16)
    projection = out_weight[0]
    out_rows = rows // lax.axis_size("head")
    summed = lax.psum_scatter(
        jnp.dot(attn, projection, preferred_element_type=jnp.float32).astype(jnp.bfloat16),
        "head",
        scatter_dimension=0,
        tiled=True,
    )
    return summed.reshape(1, out_rows, model_width)


def solution(mesh):
    placed = (
        P("tower", ("seq", "head"), None, None),
        P("tower", "head", None),
        P("tower", "seq", None),
    )
    return jax.shard_map(
        on_device,
        mesh=mesh,
        in_specs=placed,
        out_specs=P("tower", ("seq", "head"), None),
        check_vma=False,
    )
```

profile of v0, /device:TPU:1, one launch (start us, length us, event | category | flops | bytes accessed | tf_op | source)
XLA Modules:
  0.0 468.4 jit_solution(12779382957593783759)
XLA Ops:
  6.5 7.7 %copy.67 = bf16[1,64,5,3072]{1,2,3,0:T(8,128)(2,1)} copy(bf16[1,64,5,3072]{3,1,2,0:T(8,128)(2,1)} %param.7) | data formatting | bytes 3932160 | tf_op args[0]
  14.3 5.8 %slice_bitcast_fusion.8 = bf16[3072,3,64]{2,1,0:T(4,128)(2,1)} fusion(bf16[64,5,3072]{0,1,2:T(8,128)(2,1)} %bitcast.141), kind=kLoop, calls=%fused_computation.62 | loop fusion | bytes 2359296
  20.0 5.5 %reshape.42 = bf16[8,2,36864]{2,1,0:T(2,128)(2,1)S(1)} reshape(bf16[3072,3,64]{2,1,0:T(4,128)(2,1)} %slice_bitcast_fusion.8) | data formatting | bytes 2359296
  25.5 24.4 %all_to_all.36 = bf16[8,2,36864]{2,1,0:T(2,128)(2,1)} all-to-all(bf16[8,2,36864]{2,1,0:T(2,128)(2,1)S(1)} %reshape.42), channel_id=1, replica_groups=mesh['tower'=2,'seq'=16,'head'=8] {'head'}, dimensions={0} | all-to-all | bytes 2359296 | tf_op jit(solution)/shard_map/all_to_all | solution.py:74
  50.0 6.6 %reshape.43 = bf16[3072,3,64]{2,1,0:T(4,128)(2,1)} reshape(bf16[8,2,36864]{2,1,0:T(2,128)(2,1)} %all_to_all.36) | data formatting | bytes 2359296
  56.6 4.2 copy.86
  61.9 5.5 %slice.39 = bf16[64,2,3072]{0,1,2:T(2,128)(2,1)} slice(bf16[64,5,3072]{0,1,2:T(8,128)(2,1)} %bitcast.142), slice={[0:64], [3:5], [0:3072]} | slice | bytes 1572864 | tf_op jit(solution)/shard_map/slice | solution.py:72
  67.4 4.3 copy.74
  72.2 16.4 %collective-permute-done = bf16[64,2,3072]{2,0,1:T(8,128)(2,1)} collective-permute-done((bf16[64,2,3072]{2,0,1:T(8,128)(2,1)}, bf16[64,2,3072]{2,0,1:T(8,128)(2,1)}, u32[]{:S(2)}, u32[]{:S(2)}) %collective-permute-start) | collective-permute-done | bytes 786464 | tf_op jit(solution)/shard_map/ppermute | solution.py:14
  88.6 4.4 copy.75
  96.0 15.1 %all_to_all.37 = bf16[8,2,24576]{2,1,0:T(2,128)(2,1)} all-to-all(bf16[8,2,24576]{2,1,0:T(2,128)(2,1)} %reshape.40), channel_id=1, replica_groups=mesh['tower'=2,'seq'=16,'head'=8] {'head'}, dimensions={0} | all-to-all | bytes 1572864 | tf_op jit(solution)/shard_map/all_to_all | solution.py:75
  114.1 4.8 %copy.90 = bf16[64,2,8,384]{3,0,2,1:T(8,128)(2,1)} copy(bf16[64,2,8,384]{0,1,3,2:T(2,128)(2,1)} %bitcast.145) | data formatting | bytes 1572864 | tf_op jit(solution)/shard_map/all_to_all | solution.py:75
  118.9 8.2 %collective-permute-start.1 = (bf16[512,2,384]{2,0,1:T(8,128)(2,1)}, bf16[512,2,384]{2,0,1:T(8,128)(2,1)}, u32[]{:S(2)}, u32[]{:S(2)}) collective-permute-start(bf16[512,2,384]{2,0,1:T(8,128)(2,1)} %bitcast.148), channel_id=1, source_target_pairs={{0,8},{8,16},{16,24},{24,32},{32,40},{40,48},{48,56},{56,64},{64,7... | collective-permute-start | bytes 2359304 | tf_op jit(solution)/shard_map/ppermute | solution.py:20
  133.4 7.9 %collective-permute-done.1 = bf16[512,2,384]{2,0,1:T(8,128)(2,1)} collective-permute-done((bf16[512,2,384]{2,0,1:T(8,128)(2,1)}, bf16[512,2,384]{2,0,1:T(8,128)(2,1)}, u32[]{:S(2)}, u32[]{:S(2)}) %collective-permute-start.1) | collective-permute-done | bytes 786464 | tf_op jit(solution)/shard_map/ppermute | solution.py:20
  146.5 7.0 %reshape.37 = bf16[3,512,2,3,128]{4,3,1,0,2:T(4,128)(2,1)} reshape(bf16[1536,2,384]{2,0,1:T(8,128)(2,1)} %pad_maximum_fusion) | data formatting | bytes 4718592 | tf_op jit(solution)/shard_map/reshape | solution.py:27
  157.5 34.3 %while.31 = (s32[]{:T(128)}, f32[3,512]{1,0:T(4,128)S(1)}, f32[3,512]{1,0:T(4,128)S(1)}, f32[512,3,128]{0,2,1:T(8,128)}, s32[3,512]{1,0:T(4,128)}, /*index=5*/bf...) while((s32[]{:T(128)}, f32[3,512]{1,0:T(4,128)S(1)}, ...), condition=%wide.region_8.9_spmd.clone, body=%wide.region_4.8_spmd.clone.sunk | while | flops 415574528 | bytes 31202504 | solution.py:60
  163.9 4.0 fusion.70
  175.2 4.2 fusion.70
  186.7 4.2 fusion.70
  191.8 32.1 %reshape.39 = bf16[16,512,2,3,128]{4,3,1,0,2:T(4,128)(2,1)} reshape(bf16[8192,2,384]{2,0,1:T(8,128)(2,1)} %all-gather.2.cloned.1.call-done) | data formatting | bytes 25165824 | tf_op jit(solution)/shard_map/reshape | solution.py:27
  224.0 12.8 %copy.72 = bf16[16,512,2,3,128]{4,1,3,2,0:T(8,128)(2,1)} copy(bf16[16,512,2,3,128]{4,3,1,0,2:T(4,128)(2,1)} %reshape.39) | data formatting | bytes 25165824
  236.8 136.0 %while.30 = (s32[]{:T(128)}, f32[3,512]{1,0:T(4,128)S(1)}, f32[3,512]{1,0:T(4,128)}, f32[512,3,128]{0,2,1:T(8,128)}, bf16[16,512,2,3,128]{4,1,3,2,0:T(8,128)(2,1...) while((s32[]{:T(128)}, f32[3,512]{1,0:T(4,128)S(1)}, f32[3,512]{1,0:T(4,128)}, ...), condition=%wide.region_3.4_spmd.clone, body=%wide.region_0.3_spmd.clone.sunk | while | flops 409543680 | bytes 26497208 | solution.py:60
  265.6 3.9 fusion.63
  377.9 83.7 %reduce-scatter.2.cloned.1.call-done = bf16[64,3072]{1,0:T(8,128)(2,1)} async-done(((bf16[512,3072]{1,0:T(8,128)(2,1)}), bf16[64,3072]{1,0:T(8,128)(2,1)}) %reduce-scatter.2.cloned.1.call-update) | async-done | bytes 393232 | tf_op jit(solution)/shard_map/reduce_scatter | solution.py:107
  (289 shorter events, 181.1 us)
Async XLA Ops:
  6.5 367.9 %copy-start = (bf16[1,384,3072]{2,1,0:T(8,128)(2,1)S(1)}, bf16[1,384,3072]{2,1,0:T(8,128)(2,1)}, u32[]{:S(2)}) copy-start(bf16[1,384,3072]{2,1,0:T(8,128)(2,1)} %param.8) | copy-start | bytes 7077892
  6.5 185.3 %all-gather.2.cloned.1.call-start = ((), (), s32[]{:S(2)}) async-start(), calls=%async_computation.3 | async-start | bytes 13369344 | tf_op jit(solution)/shard_map/all_gather | solution.py:91
  61.9 399.7 %reduce-scatter.2.cloned.1.call-start = ((), (), s32[]{:S(2)}) async-start(), calls=%async_computation.4 | async-start | bytes 3538944 | tf_op jit(solution)/shard_map/reduce_scatter | solution.py:107
  71.7 16.8 %collective-permute-start = (bf16[64,2,3072]{2,0,1:T(8,128)(2,1)}, bf16[64,2,3072]{2,0,1:T(8,128)(2,1)}, u32[]{:S(2)}, u32[]{:S(2)}) collective-permute-start(bf16[64,2,3072]{2,0,1:T(8,128)(2,1)} %copy.74), channel_id=1, source_target_pairs={{0,128},{128,0},{1,129},{129,1},{2,130},{130,2},{3,131},{131,3},{4... | collective-permute-start | bytes 2359304 | tf_op jit(solution)/shard_map/ppermute | solution.py:14
  118.9 22.4 %collective-permute-start.1 = (bf16[512,2,384]{2,0,1:T(8,128)(2,1)}, bf16[512,2,384]{2,0,1:T(8,128)(2,1)}, u32[]{:S(2)}, u32[]{:S(2)}) collective-permute-start(bf16[512,2,384]{2,0,1:T(8,128)(2,1)} %bitcast.148), channel_id=1, source_target_pairs={{0,8},{8,16},{16,24},{24,32},{32,40},{40,48},{48,56},{56,64},{64,7... | collective-permute-start | bytes 2359304 | tf_op jit(solution)/shard_map/ppermute | solution.py:20
  127.1 16.2 %collective-permute-start.2 = (bf16[512,2,384]{2,0,1:T(8,128)(2,1)}, bf16[512,2,384]{2,0,1:T(8,128)(2,1)}, u32[]{:S(2)}, u32[]{:S(2)}) collective-permute-start(bf16[512,2,384]{2,0,1:T(8,128)(2,1)} %bitcast.149), channel_id=1, source_target_pairs={{8,0},{16,8},{24,16},{32,24},{40,32},{48,40},{56,48},{64,56},{72,6... | collective-permute-start | bytes 2359304 | tf_op jit(solution)/shard_map/ppermute | solution.py:20
  175.2 4.2 copy-start.2
  191.8 32.2 %copy-start.7 = (f32[3,512]{1,0:T(4,128)}, f32[3,512]{1,0:T(4,128)S(1)}, u32[]{:S(2)}) copy-start(f32[3,512]{1,0:T(4,128)S(1)} %get-tuple-element.84) | copy-start | bytes 18436
  240.2 4.3 copy-start.4
  248.5 4.5 copy-start.4
  257.1 4.5 copy-start.4
  265.6 4.5 copy-start.4
  274.1 4.5 copy-start.4
  282.6 4.5 copy-start.4
  291.1 4.5 copy-start.4
  299.6 4.5 copy-start.4
  308.1 4.5 copy-start.4
  316.7 4.5 copy-start.4
  325.2 4.5 copy-start.4
  333.7 4.5 copy-start.4
  342.2 4.5 copy-start.4
  350.7 4.5 copy-start.4
  359.2 4.5 copy-start.4
  367.7 4.5 copy-start.4
  (39 other events, 91.1 us)
Sparse Core Ops, SparseCore 0:
  62.0 76.6 all-gather.1
  378.0 83.4 reduce-scatter.1
where the time goes:
time: 472 us; the launch traced here: 468 us
  local copies, waits for them, and re-layouts  153 us (32%)
  matrix products  121 us (26%)
  waiting for transfers between devices  110 us (23%)
  blocking collectives  39.5 us (8%)
  other arithmetic  19.3 us (4%)
  between operations  13.6 us (3%)
  starting transfers between devices  10.8 us (2%)
    reduce_scatter x1, waiting for transfers between devices, on_device(): lax.psum_scatter(jnp.dot(attn, projection, preferred_element_type=jnp.flo...  83.7 us
    dot_general x19, matrix products, advance(): jnp.einsum('hqk,khd->qhd', weights.astype(jnp.bfloat16), tile[:, 1], pref...  74.9 us
    unnamed x18, local copies, waits for them, and re-layouts  50 us
    dot_general x19, matrix products, advance(): jnp.einsum('qhd,khd->hqk', queries, tile[:, 0], preferred_element_type=jn...  42.7 us
    reshape x2, local copies, waits for them, and re-layouts, attend_piece(): tiles = piece.reshape(count // step_rows, step_rows, 2, heads_dev, DH)  39.1 us
    all_to_all x1, blocking collectives, on_device(): lax.all_to_all(local[:, 0:3], 'head', split_axis=2, concat_axis=0, tiled=...  24.4 us
    squeeze x19, local copies, waits for them, and re-layouts, attend_piece(): result, unused = lax.scan(advance, carry, (tiles, tile_ids))  22.5 us
    ppermute x1, waiting for transfers between devices, from_partner(): return lax.ppermute(value, axis, pairs)  16.4 us
  transfers between devices with their start and end apart: 5, of which 4 were waited for; matrix products, arithmetic and copies ran while one was open for 16% of the time, Pallas kernels for 0%

commit v1 on v0

v1 whole, which is shorter than its diff:
```python
import functools
import math

import jax
import jax.numpy as jnp
from jax import lax
from jax.experimental import pallas as pl
from jax.experimental.pallas import tpu as pltpu
from jax.sharding import PartitionSpec as P

DH = 128
SCALE = math.log2(math.e) / math.sqrt(DH)
LOW = -1e30
LAG = 2
MESH = pl.DeviceIdType.MESH
VMEM_BYTES = 56 * 1024 * 1024


def order_of(half):
    phases = [["own"]]
    for k in range(1, half):
        before = ["sown"] if k == 1 else [f"sl{k - 1}", f"sr{k - 1}"]
        phases.append([f"l{k}", f"r{k}"] + before)
    before = ["sown"] if half == 1 else [f"sl{half - 1}", f"sr{half - 1}"]
    phases.append(["x"] + before + ["sx"])
    flat = [name for phase in phases for name in phase]
    ends = []
    for phase in phases:
        ends.append((ends[-1] if ends else 0) + len(phase))
    return {name: i for i, name in enumerate(flat)}, ends


def pick(index, values):
    result = values[0]
    for i, value in enumerate(values[1:], 1):
        result = jnp.where(index == i, value, result)
    return result


def kernel(sizes, acts, weight, pairs, out, kv, q, kvx, acc, peak, cross, attn, wv, psend, prec,
           a_send, a_recv, q_send, q_recv, x_send, x_recv, g_send, g_recv, h_send, h_recv,
           r_send, r_recv, l_sem):
    n_head, n_seq, heads, cols = sizes
    rows = acts.shape[1]
    span = rows * n_head
    blk = span // 2
    width = heads * DH
    model = out.shape[1]
    half = n_seq // 4
    place, ends = order_of(half)
    n_pos = len(place)
    n_cols = model // cols

    t, s, me = lax.axis_index("tower"), lax.axis_index("seq"), lax.axis_index("head")
    core = s % 2
    sib = s + 1 - 2 * core
    up, down = (s + 2) % n_seq, (s + n_seq - 2) % n_seq
    nxt, prv = (s + 1) % n_seq, (s + n_seq - 1) % n_seq
    far = jnp.where(core == 0, prv, nxt)

    def head_of(j):
        return (me + j) % n_head

    partners = [(t, s, head_of(j)) for j in range(1, n_head)]
    partners += [(1 - t, s, head_of(j)) for j in range(n_head)]
    partners += [(t, up, me), (t, down, me), (t, sib, me), (t, far, me)]
    barrier = pltpu.get_barrier_semaphore()
    for device in partners:
        pl.semaphore_signal(barrier, inc=1, device_id=device, device_id_type=MESH)

    def at(index, size):
        return pl.ds(pl.multiple_of(index * size, size), size)

    def remote(src, dst, send, recv, device):
        return pltpu.make_async_remote_copy(
            src_ref=src, dst_ref=dst, send_sem=send, recv_sem=recv, device_id=device, device_id_type=MESH)

    def kv_out(h, j):
        src = acts.at[pl.ds(1, 2), :, at(head_of(j) * heads + h, DH)]
        dst = kv.at[place["own"], h, :, at(me, rows), :]
        if j == 0:
            return pltpu.make_async_copy(src, dst, l_sem.at[h])
        return remote(src, dst, a_send.at[h, j], a_recv.at[h, j], (t, s, head_of(j)))

    def q_out(j):
        src, dst = acts.at[0, :, at(head_of(j), width)], q.at[at(me, rows), :]
        if j == 0:
            return pltpu.make_async_copy(src, dst, l_sem.at[heads])
        return remote(src, dst, q_send.at[j], q_recv.at[j], (t, s, head_of(j)))

    def x_out(j):
        src = acts.at[pl.ds(3, 2), :, at(head_of(j), width)]
        dst = kvx.at[:, pl.ds(pl.multiple_of(blk + me * rows, rows), rows), :]
        return remote(src, dst, x_send.at[j], x_recv.at[j], (1 - t, s, head_of(j)))

    def halo_out(way):
        src = kvx.at[:, pl.ds(2 * blk if way == 0 else blk, blk), :]
        dst = kvx.at[:, pl.ds(0 if way == 0 else 3 * blk, blk), :]
        return remote(src, dst, h_send.at[way], h_recv.at[way], (t, nxt if way == 0 else prv, me))

    def ring(h, source, target, device, part=None):
        rows_of = pl.ds(0, span) if part is None else pl.ds(part * blk, blk)
        sem = n_pos if part == 1 else place[target]
        return remote(kv.at[place[source], h, :, rows_of, :], kv.at[place[target], h, :, rows_of, :],
                      g_send.at[h, sem], g_recv.at[h, sem], device)

    def forwards(name):
        result = []
        if name[0] == "s":
            return result
        distance = 0 if name == "own" else half if name == "x" else int(name[1:])
        for way, device, part in (("l", (t, up, me), 0), ("r", (t, down, me), 1)):
            if name == "own" or name[0] == way:
                if distance + 1 < half:
                    result.append((name, f"{way}{distance + 1}", device, None))
                elif distance + 1 == half:
                    result.append((name, "x", device, part))
        result.append((name, "s" + name, (t, sib, me), None))
        return result

    def arrive(h, name):
        if name == "own":
            kv_out(h, 0).wait()
            for j in range(1, n_head):
                kv_out(h, j).wait_recv()
        elif name == "x":
            ring(h, "x", "x", (t, up, me), 0).wait_recv()
            ring(h, "x", "x", (t, down, me), 1).wait_recv()
        else:
            ring(h, name, name, (t, sib, me)).wait_recv()

    ones = jnp.ones((span, DH), jnp.bfloat16)

    def wide(value, times):
        return jnp.concatenate([value] * times, axis=1)

    def attend(h, pos):
        keys = kv[pos, h, 0]
        values = jnp.concatenate([kv[pos, h, 1], ones], axis=1)
        lanes = at(h, DH)
        for part in range(2):
            at_rows = pl.ds(part * blk, blk)
            scores = lax.dot_general(q[at_rows, lanes], keys, (((1,), (1,)), ((), ())),
                                     preferred_element_type=jnp.float32)
            old = peak[h, at_rows]
            new = jnp.maximum(old, jnp.max(scores, axis=1, keepdims=True))
            weights = jnp.exp2((scores - wide(new, span // DH)) * SCALE).astype(jnp.bfloat16)
            shrink = jnp.exp2((old - new) * SCALE)
            update = jnp.dot(weights, values, preferred_element_type=jnp.float32)
            acc[h, at_rows] = acc[h, at_rows] * wide(shrink, 2) + update
            peak[h, at_rows] = new

    def attend_cross(h, part):
        lanes = at(h, DH)
        at_rows, at_keys = at(part, blk), pl.ds(pl.multiple_of(part * blk, blk), 3 * blk)
        scores = lax.dot_general(q[at_rows, lanes], kvx[0, at_keys, lanes], (((1,), (1,)), ((), ())),
                                 preferred_element_type=jnp.float32)
        pieces = []
        for slot in range(3):
            shift = jnp.where(pairs[part, slot] >= 0, 0.0, LOW)
            pieces.append(scores[:, slot * blk:(slot + 1) * blk] + shift)
        scores = jnp.concatenate(pieces, axis=1)
        top = jnp.max(scores, axis=1, keepdims=True)
        weights = jnp.exp2((scores - top) * SCALE).astype(jnp.bfloat16)
        values = jnp.concatenate([kvx[1, at_keys, lanes], jnp.ones((3 * blk, DH), jnp.bfloat16)], axis=1)
        result = jnp.dot(weights, values, preferred_element_type=jnp.float32)
        cross[at_rows, lanes] = result[:, :DH] / result[:, DH:]

    weight_copy = pltpu.make_async_copy(weight, wv, l_sem.at[heads + 1])
    weight_copy.start()
    for h in range(heads):
        acc[h] = jnp.zeros((span, 2 * DH), jnp.float32)
        peak[h] = jnp.full((span, DH), LOW, jnp.float32)
    pl.semaphore_wait(barrier, len(partners))
    for h in range(heads):
        for j in range(n_head):
            kv_out(h, j).start()
        if h == 0:
            for j in range(n_head):
                q_out(j).start()
    for j in range(n_head):
        x_out(j).start()

    n_phases = len(ends)

    def advance(i, carry):
        tick, h = i // heads, i % heads
        phase = tick - LAG * h
        names = sorted(place, key=place.get)
        starts = [0] + ends[:-1]
        for at_phase in range(n_phases):
            @pl.when(phase == at_phase)
            def _():
                for name in names[starts[at_phase]:ends[at_phase]]:
                    arrive(h, name)
                    for hop in forwards(name):
                        ring(h, *hop).start()
                if at_phase == 0:
                    @pl.when(h == 0)
                    def _():
                        q_out(0).wait()
                        for j in range(1, n_head):
                            q_out(j).wait_recv()

        @pl.when((phase >= 0) & (phase < n_phases))
        def _():
            def step(pos, inner):
                attend(h, pos)
                return inner

            lax.fori_loop(pick(phase, starts), pick(phase, ends), step, 0)

        @pl.when((phase == 1) & (h == 0))
        def _():
            for j in range(n_head):
                x_out(j).wait_recv()
            halo_out(0).start()
            halo_out(1).start()

        @pl.when((phase == n_phases - 1) & (h == 0))
        def _():
            halo_out(0).wait_recv()
            halo_out(1).wait_recv()

            def step(index, inner):
                attend_cross(index // 2, index % 2)
                return inner

            lax.fori_loop(0, 2 * heads, step, 0)

        @pl.when(phase == n_phases - 1)
        def _():
            lanes = at(h, DH)
            self_out = acc[h, :, pl.ds(0, DH)] / acc[h, :, pl.ds(DH, DH)]
            attn[:, lanes] = (self_out + cross[:, lanes]).astype(jnp.bfloat16)

        return carry

    lax.fori_loop(0, heads * (n_phases + LAG * (heads - 1)), advance, 0)

    def share_out(n, j):
        where = at(n, cols)
        return remote(psend.at[at(head_of(j), rows), where], prec.at[j, :, where],
                      r_send.at[n, j], r_recv.at[n, j], (t, s, head_of(j)))

    weight_copy.wait()

    def project(n, carry):
        where = at(n, cols)
        psend[:, where] = jnp.dot(attn[...], wv[:, where], preferred_element_type=jnp.float32).astype(jnp.bfloat16)
        for j in range(1, n_head):
            share_out(n, j).start()
        return carry

    lax.fori_loop(0, n_cols, project, 0)

    def collect(n, carry):
        where = at(n, cols)
        total = psend[at(me, rows), where].astype(jnp.float32)
        for j in range(1, n_head):
            share_out(n, j).wait_recv()
            total = total + prec[j, :, where].astype(jnp.float32)
        out[:, where] = total.astype(jnp.bfloat16)
        return carry

    lax.fori_loop(0, n_cols, collect, 0)

    def drain(h, carry):
        for j in range(1, n_head):
            kv_out(h, j).wait_send()
        for name in place:
            for hop in forwards(name):
                ring(h, *hop).wait_send()
        return carry

    lax.fori_loop(0, heads, drain, 0)
    for j in range(n_head):
        if j:
            q_out(j).wait_send()
        x_out(j).wait_send()
    halo_out(0).wait_send()
    halo_out(1).wait_send()

    def drain_shares(n, carry):
        for j in range(1, n_head):
            share_out(n, j).wait_send()
        return carry

    lax.fori_loop(0, n_cols, drain_shares, 0)


def on_device(mesh_shape, acts, out_weight, pairs):
    n_head, n_seq = mesh_shape["head"], mesh_shape["seq"]
    rows, model = acts.shape[1], acts.shape[3]
    width = out_weight.shape[1]
    heads, span = width // DH, rows * n_head
    cols = math.gcd(model, 512)
    n_cols = model // cols
    n_pos = n_seq
    dma = pltpu.SemaphoreType.DMA
    bf16, f32 = jnp.bfloat16, jnp.float32
    result = pl.pallas_call(
        functools.partial(kernel, (n_head, n_seq, heads, cols)),
        out_shape=jax.ShapeDtypeStruct((rows, model), bf16),
        in_specs=[pl.BlockSpec(memory_space=pl.ANY), pl.BlockSpec(memory_space=pl.ANY),
                  pl.BlockSpec(memory_space=pltpu.SMEM)],
        out_specs=pl.BlockSpec(memory_space=pltpu.VMEM),
        scratch_shapes=[
            pltpu.VMEM((n_pos, heads, 2, span, DH), bf16),
            pltpu.VMEM((span, width), bf16),
            pltpu.VMEM((2, 2 * span, width), bf16),
            pltpu.VMEM((heads, span, 2 * DH), f32),
            pltpu.VMEM((heads, span, DH), f32),
            pltpu.VMEM((span, width), f32),
            pltpu.VMEM((span, width), bf16),
            pltpu.VMEM((width, model), bf16),
            pltpu.VMEM((span, model), bf16),
            pltpu.VMEM((n_head, rows, model), bf16),
            dma((heads, n_head)), dma((heads, n_head)),
            dma((n_head,)), dma((n_head,)),
            dma((n_head,)), dma((n_head,)),
            dma((heads, n_pos + 1)), dma((heads, n_pos + 1)),
            dma((2,)), dma((2,)),
            dma((n_cols, n_head)), dma((n_cols, n_head)),
            dma((heads + 2,)),
        ],
        compiler_params=pltpu.CompilerParams(
            collective_id=0, has_side_effects=True, vmem_limit_bytes=VMEM_BYTES),
        cost_estimate=pl.CostEstimate(flops=10**10, bytes_accessed=2 * 10**7, transcendentals=10**7),
    )(jnp.transpose(acts[0], (1, 0, 2)), out_weight[0], pairs[0])
    return result[None]


def solution(mesh):
    placed = (
        P("tower", ("seq", "head"), None, None),
        P("tower", "head", None),
        P("tower", "seq", None),
    )
    return jax.shard_map(
        functools.partial(on_device, dict(mesh.shape)),
        mesh=mesh,
        in_specs=placed,
        out_specs=P("tower", ("seq", "head"), None),
        check_vma=False,
    )
```

time: 472 us -> 148 us (0.31)
  local copies, waits for them, and re-layouts: 153 us -> 1.77 us
  Pallas kernels: 0 us -> 146 us
  matrix products: 121 us -> 0 us
  waiting for transfers between devices: 110 us -> 0 us
  blocking collectives: 39.5 us -> 0 us
  other arithmetic: 19.3 us -> 0 us
  between operations: 13.6 us -> 0.01 us
  starting transfers between devices: 10.8 us -> 0 us
    pallas_call x0 -> x1, Pallas kernels: none -> 146 us  [on_device(): pl.pallas_call(functools.partial(kernel, (n_head, n_seq, heads, cols)), o...]
    dot_general x39 -> x0, matrix products: 121 us -> none  [the longest x19 74.9 us: advance(): jnp.einsum('hqk,khd->qhd', weights.astype(jnp.bfloat16), tile[:, 1], pref...]
    reduce_scatter x1 -> x0, waiting for transfers between devices: 83.7 us -> none  [on_device(): lax.psum_scatter(jnp.dot(attn, projection, preferred_element_type=jnp.flo...]
    unnamed x18 -> x1, local copies, waits for them, and re-layouts: 50 us -> 1.77 us
    all_to_all x2 -> x0, blocking collectives: 39.5 us -> none  [the longest x1 24.4 us: on_device(): lax.all_to_all(local[:, 0:3], 'head', split_axis=2, concat_axis=0, tiled=...]
    reshape x2 -> x0, local copies, waits for them, and re-layouts: 39.1 us -> none  [attend_piece(): tiles = piece.reshape(count // step_rows, step_rows, 2, heads_dev, DH)]
    ppermute x3 -> x0, waiting for transfers between devices: 26.2 us -> none  [the longest x1 16.4 us: from_partner(): return lax.ppermute(value, axis, pairs)]
    squeeze x19 -> x0, local copies, waits for them, and re-layouts: 22.5 us -> none  [attend_piece(): result, unused = lax.scan(advance, carry, (tiles, tile_ids))]
  transfers between devices with their start and end apart: 5 -> 0, of which waited for: 4 -> 0; matrix products, arithmetic and copies ran while one was open for 16% -> 0% of each run, Pallas kernels for 0% -> 0%
where the time goes in v1:
time: 148 us
  Pallas kernels  146 us (99%)
  local copies, waits for them, and re-layouts  1.77 us (1%)
    pallas_call x1, Pallas kernels, on_device(): pl.pallas_call(functools.partial(kernel, (n_head, n_seq, heads, cols)), o...  146 us

profile of v1, /device:TPU:1, one launch (start us, length us, event | category | flops | bytes accessed | tf_op | source)
XLA Modules:
  0.0 148.0 jit_solution(14366031039723558017)
XLA Ops:
  0.0 146.2 %shard_map.37 = bf16[64,3072]{1,0:T(8,128)(2,1)} custom-call(bf16[5,64,3072]{2,1,0:T(8,128)(2,1)} %bitcast.8, bf16[384,3072]{1,0:T(8,128)(2,1)} %bitcast.7, s32[2,3]{1,0:T(2,128)} %bitcast.9), custom_call_target="tpu_custom_call" | custom-call | flops 10000000000 | bytes 20000000 | tf_op jit(solution)/shard_map/pallas_call | solution.py:302
  146.2 1.8 %copy.5 = bf16[1,64,3072]{2,1,0:T(8,128)(2,1)} copy(bf16[1,64,3072]{2,1,0:T(8,128)(2,1)} %bitcast.6) | data formatting | bytes 786432

commit v2 on v1

--- a/solution.py
+++ b/solution.py
@@ -11,7 +11,8 @@
 DH = 128
 SCALE = math.log2(math.e) / math.sqrt(DH)
 LOW = -1e30
-LAG = 2
+LAG = 1
+N_Y = 4
 MESH = pl.DeviceIdType.MESH
 VMEM_BYTES = 56 * 1024 * 1024
 
@@ -22,7 +23,7 @@
         before = ["sown"] if k == 1 else [f"sl{k - 1}", f"sr{k - 1}"]
         phases.append([f"l{k}", f"r{k}"] + before)
     before = ["sown"] if half == 1 else [f"sl{half - 1}", f"sr{half - 1}"]
-    phases.append(["x"] + before + ["sx"])
+    phases.append(before + ["x", "sx"])
     flat = [name for phase in phases for name in phase]
     ends = []
     for phase in phases:
@@ -37,9 +38,9 @@
     return result
 
 
-def kernel(sizes, acts, weight, pairs, out, kv, q, kvx, acc, peak, cross, attn, wv, psend, prec,
+def kernel(sizes, acts, weight, pairs, out, kv, q, kvx, acc, peak, cross, attn, near, wv, total, give, take,
            a_send, a_recv, q_send, q_recv, x_send, x_recv, g_send, g_recv, h_send, h_recv,
-           r_send, r_recv, l_sem):
+           w_send, w_recv, y_send, y_recv, r_send, r_recv, l_sem):
     n_head, n_seq, heads, cols = sizes
     rows = acts.shape[1]
     span = rows * n_head
@@ -57,6 +58,8 @@
     up, down = (s + 2) % n_seq, (s + n_seq - 2) % n_seq
     nxt, prv = (s + 1) % n_seq, (s + n_seq - 1) % n_seq
     far = jnp.where(core == 0, prv, nxt)
+    x_at, y_at = me // N_Y, me % N_Y
+    w_cols = model // 2
 
     def head_of(j):
         return (me + j) % n_head
@@ -166,8 +169,100 @@
         result = jnp.dot(weights, values, preferred_element_type=jnp.float32)
         cross[at_rows, lanes] = result[:, :DH] / result[:, DH:]
 
-    weight_copy = pltpu.make_async_copy(weight, wv, l_sem.at[heads + 1])
-    weight_copy.start()
+    def along_y(j):
+        return (t, s, x_at * N_Y + (y_at + j) % N_Y)
+
+    def w_own(h):
+        return pltpu.make_async_copy(weight.at[h], wv.at[h, pl.ds(0, DH)], l_sem.at[heads + 1 + h])
+
+    def w_part(slot, owner, part=None):
+        size = w_cols if part is None else w_cols // 2
+        start = owner * w_cols + (0 if part is None else part * size)
+        return pl.ds(slot * DH, DH), pl.ds(pl.multiple_of(start, size), size)
+
+    def w_out(h, way):
+        into, where = w_part(1 if way == 0 else N_Y - 1, core)
+        return remote(weight.at[h, :, where], wv.at[h, into, where],
+                      w_send.at[h, way], w_recv.at[h, way], along_y(1 if way == 0 else N_Y - 1))
+
+    def w_on(h, way):
+        rows_of, where = w_part(1 if way == 0 else N_Y - 1, core, way)
+        into, unused = w_part(2, core, way)
+        return remote(wv.at[h, rows_of, where], wv.at[h, into, where],
+                      w_send.at[h, 2 + way], w_recv.at[h, 2 + way], along_y(1 if way == 0 else N_Y - 1))
+
+    def w_over(h, slot, owner):
+        rows_of, where = w_part(slot, owner)
+        return remote(wv.at[h, rows_of, where], wv.at[h, rows_of, where],
+                      w_send.at[h, 3 + slot], w_recv.at[h, 3 + slot], (t, sib, me))
+
+    def w_first(h):
+        w_own(h).start()
+        w_out(h, 0).start()
+        w_out(h, 1).start()
+
+    def w_second(h):
+        for way, slot in ((0, 1), (1, N_Y - 1)):
+            w_out(h, way).wait_recv()
+            w_on(h, way).start()
+            w_over(h, slot, core).start()
+
+    def w_third(h):
+        w_on(h, 0).wait_recv()
+        w_on(h, 1).wait_recv()
+        w_over(h, 2, core).start()
+
+    def attn_out(h, j):
+        lanes = pl.ds(h * DH, DH)
+        return remote(attn.at[:, (y_at + j) % N_Y, :, lanes], near.at[h, :, :, pl.ds(j * DH, DH)],
+                      y_send.at[h, j], y_recv.at[h, j], along_y(j))
+
+    def share_out(n):
+        return remote(give.at[:, at(n, cols)], take.at[:, at(n, cols)], r_send.at[n], r_recv.at[n],
+                      (t, s, (1 - x_at) * N_Y + y_at))
+
+    def project(h):
+        w_own(h).wait()
+        for j in range(1, N_Y):
+            attn_out(h, j).wait_recv()
+            w_over(h, j, 1 - core).wait_recv()
+        near[h, :, :, pl.ds(0, DH)] = attn[:, y_at, :, pl.ds(h * DH, DH)]
+        mine = near[h].reshape(2 * rows, N_Y * DH)
+
+        def step(n, carry):
+            where = at(n, cols)
+            value = jnp.dot(mine, wv[h, :, where], preferred_element_type=jnp.float32)
+            if h:
+                value = value + total[:, where]
+            total[:, where] = value
+            if h == heads - 1:
+                give[:, where] = total[at(1 - x_at, rows), where].astype(jnp.bfloat16)
+                share_out(n).start()
+            return carry
+
+        lax.fori_loop(0, n_cols, step, 0)
+
+    def cross_of(h):
+        def step(part, carry):
+            attend_cross(h, part)
+            return carry
+
+        lax.fori_loop(0, 2, step, 0)
+
+    def x_first():
+        for j in range(n_head):
+            x_out(j).start()
+
+    def x_second():
+        for j in range(n_head):
+            x_out(j).wait_recv()
+        halo_out(0).start()
+        halo_out(1).start()
+
+    def x_third():
+        halo_out(0).wait_recv()
+        halo_out(1).wait_recv()
+
     for h in range(heads):
         acc[h] = jnp.zeros((span, 2 * DH), jnp.float32)
         peak[h] = jnp.full((span, DH), LOW, jnp.float32)
@@ -178,23 +273,41 @@
         if h == 0:
             for j in range(n_head):
                 q_out(j).start()
-    for j in range(n_head):
-        x_out(j).start()
-
     n_phases = len(ends)
+    final = heads * (n_phases - 1)
+    events = [
+        (min(3, final), x_first), (min(3, final + 3), lambda: w_first(0)),
+        (min(6, final + 3), lambda: w_second(0)), (min(6, final + 3), lambda: w_first(1)),
+        (min(7, final), x_second),
+        (min(8, final + 3), lambda: w_first(2)),
+        (min(9, final + 3), lambda: w_second(1)), (min(9, final + 3), lambda: w_third(0)),
+        (min(10, final), x_third), (min(10, final), lambda: cross_of(0)),
+        (min(11, final + 3), lambda: w_second(2)), (min(11, final + 3), lambda: w_third(1)),
+        (min(13, final + 3), lambda: cross_of(1)), (min(13, final + 3), lambda: w_third(2)),
+        (final + 4, lambda: project(0)), (final + 5, lambda: cross_of(2)),
+        (final + 6, lambda: project(1)),
+    ]
 
     def advance(i, carry):
         tick, h = i // heads, i % heads
         phase = tick - LAG * h
         names = sorted(place, key=place.get)
         starts = [0] + ends[:-1]
-        for at_phase in range(n_phases):
+        for when in sorted({event[0] for event in events}):
+            @pl.when(i == when)
+            def _():
+                for event in events:
+                    if event[0] == when:
+                        event[1]()
+
+        for at_phase in range(n_phases - 1):
             @pl.when(phase == at_phase)
             def _():
                 for name in names[starts[at_phase]:ends[at_phase]]:
-                    arrive(h, name)
-                    for hop in forwards(name):
-                        ring(h, *hop).start()
+                    if name[0] != "s":
+                        arrive(h, name)
+                        for hop in forwards(name):
+                            ring(h, *hop).start()
                 if at_phase == 0:
                     @pl.when(h == 0)
                     def _():
@@ -204,63 +317,45 @@
 
         @pl.when((phase >= 0) & (phase < n_phases))
         def _():
+            first = pick(phase, starts)
+            opposite = place["x"]
+            passed = first + jnp.where(phase == 0, 1, jnp.where(phase == n_phases - 1, 0, 2))
+
             def step(pos, inner):
+                @pl.when(pos == opposite)
+                def _():
+                    arrive(h, "x")
+                    for hop in forwards("x"):
+                        ring(h, *hop).start()
+
+                @pl.when((pos >= passed) & (pos != opposite))
+                def _():
+                    remote(kv.at[pos, h], kv.at[pos, h], g_send.at[h, pos], g_recv.at[h, pos], (t, sib, me)).wait_recv()
+
                 attend(h, pos)
                 return inner
 
-            lax.fori_loop(pick(phase, starts), pick(phase, ends), step, 0)
-
-        @pl.when((phase == 1) & (h == 0))
-        def _():
-            for j in range(n_head):
-                x_out(j).wait_recv()
-            halo_out(0).start()
-            halo_out(1).start()
-
-        @pl.when((phase == n_phases - 1) & (h == 0))
-        def _():
-            halo_out(0).wait_recv()
-            halo_out(1).wait_recv()
-
-            def step(index, inner):
-                attend_cross(index // 2, index % 2)
-                return inner
-
-            lax.fori_loop(0, 2 * heads, step, 0)
-
-        @pl.when(phase == n_phases - 1)
-        def _():
-            lanes = at(h, DH)
-            self_out = acc[h, :, pl.ds(0, DH)] / acc[h, :, pl.ds(DH, DH)]
-            attn[:, lanes] = (self_out + cross[:, lanes]).astype(jnp.bfloat16)
+            lax.fori_loop(first, pick(phase, ends), step, 0)
+
+        for at_head in range(heads):
+            @pl.when((phase == n_phases - 1) & (h == at_head))
+            def _():
+                lanes = pl.ds(at_head * DH, DH)
+                self_out = acc[at_head, :, pl.ds(0, DH)] / acc[at_head, :, pl.ds(DH, DH)]
+                value = (self_out + cross[:, lanes]).astype(jnp.bfloat16)
+                attn[:, :, :, lanes] = value.reshape(2, N_Y, rows, DH)
+                for j in range(1, N_Y):
+                    attn_out(at_head, j).start()
 
         return carry
 
     lax.fori_loop(0, heads * (n_phases + LAG * (heads - 1)), advance, 0)
-
-    def share_out(n, j):
-        where = at(n, cols)
-        return remote(psend.at[at(head_of(j), rows), where], prec.at[j, :, where],
-                      r_send.at[n, j], r_recv.at[n, j], (t, s, head_of(j)))
-
-    weight_copy.wait()
-
-    def project(n, carry):
-        where = at(n, cols)
-        psend[:, where] = jnp.dot(attn[...], wv[:, where], preferred_element_type=jnp.float32).astype(jnp.bfloat16)
-        for j in range(1, n_head):
-            share_out(n, j).start()
-        return carry
-
-    lax.fori_loop(0, n_cols, project, 0)
+    project(heads - 1)
 
     def collect(n, carry):
         where = at(n, cols)
-        total = psend[at(me, rows), where].astype(jnp.float32)
-        for j in range(1, n_head):
-            share_out(n, j).wait_recv()
-            total = total + prec[j, :, where].astype(jnp.float32)
-        out[:, where] = total.astype(jnp.bfloat16)
+        share_out(n).wait_recv()
+        out[:, where] = (total[at(x_at, rows), where] + take[:, where].astype(jnp.float32)).astype(jnp.bfloat16)
         return carry
 
     lax.fori_loop(0, n_cols, collect, 0)
@@ -281,9 +376,16 @@
     halo_out(0).wait_send()
     halo_out(1).wait_send()
 
+    for h in range(heads):
+        for way in range(2):
+            w_out(h, way).wait_send()
+            w_on(h, way).wait_send()
+        for j in range(1, N_Y):
+            w_over(h, j, core).wait_send()
+            attn_out(h, j).wait_send()
+
     def drain_shares(n, carry):
-        for j in range(1, n_head):
-            share_out(n, j).wait_send()
+        share_out(n).wait_send()
         return carry
 
     lax.fori_loop(0, n_cols, drain_shares, 0)
@@ -312,22 +414,26 @@
             pltpu.VMEM((heads, span, 2 * DH), f32),
             pltpu.VMEM((heads, span, DH), f32),
             pltpu.VMEM((span, width), f32),
-            pltpu.VMEM((span, width), bf16),
-            pltpu.VMEM((width, model), bf16),
-            pltpu.VMEM((span, model), bf16),
-            pltpu.VMEM((n_head, rows, model), bf16),
+            pltpu.VMEM((2, N_Y, rows, width), bf16),
+            pltpu.VMEM((heads, 2, rows, N_Y * DH), bf16),
+            pltpu.VMEM((heads, N_Y * DH, model), bf16),
+            pltpu.VMEM((2 * rows, model), f32),
+            pltpu.VMEM((rows, model), bf16),
+            pltpu.VMEM((rows, model), bf16),
             dma((heads, n_head)), dma((heads, n_head)),
             dma((n_head,)), dma((n_head,)),
             dma((n_head,)), dma((n_head,)),
             dma((heads, n_pos + 1)), dma((heads, n_pos + 1)),
             dma((2,)), dma((2,)),
-            dma((n_cols, n_head)), dma((n_cols, n_head)),
-            dma((heads + 2,)),
+            dma((heads, 4 + N_Y)), dma((heads, 4 + N_Y)),
+            dma((heads, N_Y)), dma((heads, N_Y)),
+            dma((n_cols,)), dma((n_cols,)),
+            dma((2 * heads + 1,)),
         ],
         compiler_params=pltpu.CompilerParams(
             collective_id=0, has_side_effects=True, vmem_limit_bytes=VMEM_BYTES),
         cost_estimate=pl.CostEstimate(flops=10**10, bytes_accessed=2 * 10**7, transcendentals=10**7),
-    )(jnp.transpose(acts[0], (1, 0, 2)), out_weight[0], pairs[0])
+    )(jnp.transpose(acts[0], (1, 0, 2)), out_weight[0].reshape(heads, DH, model), pairs[0])
     return result[None]
 
 

time: 148 us -> 120 us (0.81)
  Pallas kernels: 146 us -> 118 us
    pallas_call x1, Pallas kernels: 146 us -> 118 us  [on_device(): pl.pallas_call(functools.partial(kernel, (n_head, n_seq, heads, cols)), o...]
where the time goes in v2:
time: 120 us
  Pallas kernels  118 us (98%)
  local copies, waits for them, and re-layouts  1.77 us (1%)
    pallas_call x1, Pallas kernels, on_device(): pl.pallas_call(functools.partial(kernel, (n_head, n_seq, heads, cols)), o...  118 us

profile of v2, /device:TPU:1, one launch (start us, length us, event | category | flops | bytes accessed | tf_op | source)
XLA Modules:
  0.0 120.0 jit_solution(1131736535117546255)
XLA Ops:
  0.0 118.2 %shard_map.37 = bf16[64,3072]{1,0:T(8,128)(2,1)} custom-call(bf16[5,64,3072]{2,1,0:T(8,128)(2,1)} %bitcast.8, bf16[3,128,3072]{2,1,0:T(8,128)(2,1)} %bitcast.7, s32[2,3]{1,0:T(2,128)} %bitcast.9), custom_call_target="tpu_custom_call" | custom-call | flops 10000000000 | bytes 20000000 | tf_op jit(solution)/shard_map/pallas_call | solution.py:404
  118.2 1.8 %copy.5 = bf16[1,64,3072]{2,1,0:T(8,128)(2,1)} copy(bf16[1,64,3072]{2,1,0:T(8,128)(2,1)} %bitcast.6) | data formatting | bytes 786432

commit v3 on v2

v3 whole, which is shorter than its diff:
```python
import functools
import math

import jax
import jax.numpy as jnp
from jax import lax
from jax.experimental import pallas as pl
from jax.experimental.pallas import tpu as pltpu
from jax.sharding import PartitionSpec as P

DH = 128
SCALE = math.log2(math.e) / math.sqrt(DH)
LOW = -1e30
LAG = 1
PARTS = 2
N_Y = 4
MESH = pl.DeviceIdType.MESH
VMEM_BYTES = 56 * 1024 * 1024


def order_of(half):
    names = ["own", "sown"]
    for k in range(1, half):
        names += [f"l{k}", f"r{k}", f"sl{k}", f"sr{k}"]
    return {name: i for i, name in enumerate(names + ["x", "sx"])}


def kernel(sizes, acts, weight, pairs, out, kv, q, kvx, acc, peak, cross, attn, near, wv, total, give, take,
           a_send, a_recv, q_send, q_recv, x_send, x_recv, g_send, g_recv, o_recv, h_send, h_recv,
           w_send, w_recv, y_send, y_recv, r_send, r_recv, l_sem):
    n_head, n_seq, heads, cols = sizes
    rows = acts.shape[1]
    span = rows * n_head
    blk = span // 2
    width = heads * DH
    model = out.shape[1]
    half = n_seq // 4
    place = order_of(half)
    stops = [name for name in place if name[0] != "s"]
    n_phases = half + 1
    n_cols = model // cols

    t, s, me = lax.axis_index("tower"), lax.axis_index("seq"), lax.axis_index("head")
    core = s % 2
    sib = s + 1 - 2 * core
    up, down = (s + 2) % n_seq, (s + n_seq - 2) % n_seq
    nxt, prv = (s + 1) % n_seq, (s + n_seq - 1) % n_seq
    far = jnp.where(core == 0, prv, nxt)
    x_at, y_at = me // N_Y, me % N_Y
    w_cols = model // 2

    def head_of(j):
        return (me + j) % n_head

    partners = [(t, s, head_of(j)) for j in range(1, n_head)]
    partners += [(1 - t, s, head_of(j)) for j in range(n_head)]
    partners += [(t, up, me), (t, down, me), (t, sib, me), (t, far, me)]
    barrier = pltpu.get_barrier_semaphore()
    for device in partners:
        pl.semaphore_signal(barrier, inc=1, device_id=device, device_id_type=MESH)

    def at(index, size):
        return pl.ds(pl.multiple_of(index * size, size), size)

    def remote(src, dst, send, recv, device):
        return pltpu.make_async_remote_copy(
            src_ref=src, dst_ref=dst, send_sem=send, recv_sem=recv, device_id=device, device_id_type=MESH)

    def landed_all(ref, sem):
        pltpu.make_async_copy(ref, ref, sem).wait()

    others = pl.ds(0, span - rows)

    def kv_out(h, j):
        src = acts.at[pl.ds(1, 2), :, at(head_of(j) * heads + h, DH)]
        dst = kv.at[place["own"], h, :, at(me, rows), :]
        if j == 0:
            return pltpu.make_async_copy(src, dst, l_sem.at[h])
        return remote(src, dst, a_send.at[0], a_recv.at[h], (t, s, head_of(j)))

    def q_out(j):
        src, dst = acts.at[0, :, at(head_of(j), width)], q.at[at(me, rows), :]
        if j == 0:
            return pltpu.make_async_copy(src, dst, l_sem.at[heads])
        return remote(src, dst, q_send.at[0], q_recv.at[0], (t, s, head_of(j)))

    def x_out(j):
        src = acts.at[pl.ds(3, 2), :, at(head_of(j), width)]
        dst = kvx.at[:, pl.ds(pl.multiple_of(blk + me * rows, rows), rows), :]
        return remote(src, dst, x_send.at[0], x_recv.at[0], (1 - t, s, head_of(j)))

    def halo_out(way):
        src = kvx.at[:, pl.ds(2 * blk if way == 0 else blk, blk), :]
        dst = kvx.at[:, pl.ds(0 if way == 0 else 3 * blk, blk), :]
        return remote(src, dst, h_send.at[0], h_recv.at[way], (t, nxt if way == 0 else prv, me))

    def ring(h, source, target, device, part=None):
        rows_of = pl.ds(0, span) if part is None else pl.ds(part * blk, blk)
        if target[0] == "s":
            landed = o_recv.at[h, stops.index(target[1:])]
        else:
            landed = g_recv.at[h, stops.index(target) - 1, 0 if part is None else part]
        return remote(kv.at[place[source], h, :, rows_of, :], kv.at[place[target], h, :, rows_of, :],
                      g_send.at[0], landed, device)

    ways = {"l": (t, up, me), "r": (t, down, me)}

    def parts_of(distance):
        if distance == half:
            return {"l": [0], "r": [1]}
        whole = [None] if PARTS == 1 else [0, 1]
        return {"l": whole, "r": whole}

    def onward(name, part=None):
        distance = 0 if name == "own" else int(name[1:])
        result = []
        for way in "lr":
            if name == "own" or name[0] == way:
                for next_part in parts_of(distance + 1)[way]:
                    if part is None or next_part == part:
                        target = "x" if distance + 1 == half else f"{way}{distance + 1}"
                        result.append((name, target, ways[way], next_part))
        return result

    def over(name):
        return (name, "s" + name, (t, sib, me))

    def pass_on(h, phase):
        if phase == 0:
            kv_out(h, 0).wait()
            landed_all(kv.at[place["own"], h, :, others, :], a_recv.at[h])
            for hop in onward("own"):
                ring(h, *hop).start()
            ring(h, *over("own")).start()
        elif phase < half:
            for k in range(PARTS):
                for way in "lr":
                    parts = parts_of(phase)[way]
                    part = parts[k] if way == "l" else parts[-1 - k]
                    name = f"{way}{phase}"
                    ring(h, name, name, ways[way], part).wait_recv()
                    for hop in onward(name, part):
                        ring(h, *hop).start()
            for way in "lr":
                ring(h, *over(f"{way}{phase}")).start()
        else:
            for way, parts in parts_of(half).items():
                for part in parts:
                    ring(h, "x", "x", ways[way], part).wait_recv()
            ring(h, *over("x")).start()
        if phase > 0:
            for name in ["own"] if phase == 1 else [f"l{phase - 1}", f"r{phase - 1}"]:
                ring(h, *over(name)).wait_recv()

    def hops():
        result = onward("own") + [over("own"), over("x")]
        for k in range(1, half):
            for way in "lr":
                result += onward(f"{way}{k}") + [over(f"{way}{k}")]
        return result

    ones = jnp.ones((2 * span, DH), jnp.bfloat16)

    def wide(value, times):
        return jnp.concatenate([value] * times, axis=1)

    def attend(h, pair):
        both = pl.ds(2 * pair, 2)
        keys = kv[both, h, 0].reshape(2 * span, DH)
        values = jnp.concatenate([kv[both, h, 1].reshape(2 * span, DH), ones], axis=1)
        lanes = at(h, DH)
        parts = [pl.ds(0, blk), pl.ds(blk, blk)]
        olds = [peak[h, part] for part in parts]
        scores = [lax.dot_general(q[part, lanes], keys, (((1,), (1,)), ((), ())),
                                  preferred_element_type=jnp.float32) for part in parts]
        results = []
        for old, score in zip(olds, scores):
            new = jnp.maximum(old, jnp.max(score, axis=1, keepdims=True))
            weights = jnp.exp2((score - wide(new, 2 * span // DH)) * SCALE).astype(jnp.bfloat16)
            update = jnp.dot(weights, values, preferred_element_type=jnp.float32)
            results.append((new, jnp.exp2((old - new) * SCALE), update))
        for part, (new, shrink, update) in zip(parts, results):
            acc[h, part] = acc[h, part] * wide(shrink, 2) + update
            peak[h, part] = new

    def attend_cross(h, part):
        lanes = at(h, DH)
        at_rows, at_keys = at(part, blk), pl.ds(pl.multiple_of(part * blk, blk), 3 * blk)
        scores = lax.dot_general(q[at_rows, lanes], kvx[0, at_keys, lanes], (((1,), (1,)), ((), ())),
                                 preferred_element_type=jnp.float32)
        pieces = []
        for slot in range(3):
            shift = jnp.where(pairs[part, slot] >= 0, 0.0, LOW)
            pieces.append(scores[:, slot * blk:(slot + 1) * blk] + shift)
        scores = jnp.concatenate(pieces, axis=1)
        top = jnp.max(scores, axis=1, keepdims=True)
        weights = jnp.exp2((scores - top) * SCALE).astype(jnp.bfloat16)
        values = jnp.concatenate([kvx[1, at_keys, lanes], jnp.ones((3 * blk, DH), jnp.bfloat16)], axis=1)
        result = jnp.dot(weights, values, preferred_element_type=jnp.float32)
        cross[at_rows, lanes] = result[:, :DH] / result[:, DH:]

    def along_y(j):
        return (t, s, x_at * N_Y + (y_at + j) % N_Y)

    def w_own(h):
        return pltpu.make_async_copy(weight.at[h], wv.at[h, pl.ds(0, DH)], l_sem.at[heads + 1 + h])

    def w_part(slot, owner, part=None):
        size = w_cols if part is None else w_cols // 2
        start = owner * w_cols + (0 if part is None else part * size)
        return pl.ds(slot * DH, DH), pl.ds(pl.multiple_of(start, size), size)

    def w_out(h, way):
        into, where = w_part(1 if way == 0 else N_Y - 1, core)
        return remote(weight.at[h, :, where], wv.at[h, into, where],
                      w_send.at[0], w_recv.at[h, way], along_y(1 if way == 0 else N_Y - 1))

    def w_on(h, way):
        rows_of, where = w_part(1 if way == 0 else N_Y - 1, core, way)
        into, unused = w_part(2, core, way)
        return remote(wv.at[h, rows_of, where], wv.at[h, into, where],
                      w_send.at[0], w_recv.at[h, 2 + way], along_y(1 if way == 0 else N_Y - 1))

    def w_over(h, slot, owner):
        rows_of, where = w_part(slot, owner)
        return remote(wv.at[h, rows_of, where], wv.at[h, rows_of, where],
                      w_send.at[0], w_recv.at[h, 3 + slot], (t, sib, me))

    def w_first(h):
        w_own(h).start()
        w_out(h, 0).start()
        w_out(h, 1).start()

    def w_second(h):
        for way, slot in ((0, 1), (1, N_Y - 1)):
            w_out(h, way).wait_recv()
            w_on(h, way).start()
            w_over(h, slot, core).start()

    def w_third(h):
        w_on(h, 0).wait_recv()
        w_on(h, 1).wait_recv()
        w_over(h, 2, core).start()

    def attn_out(h, j):
        lanes = pl.ds(h * DH, DH)
        return remote(attn.at[:, (y_at + j) % N_Y, :, lanes], near.at[h, :, :, pl.ds(j * DH, DH)],
                      y_send.at[0], y_recv.at[h], along_y(j))

    def share_out(n):
        return remote(give.at[:, at(n, cols)], take.at[:, at(n, cols)], r_send.at[0], r_recv.at[n],
                      (t, s, (1 - x_at) * N_Y + y_at))

    def project(h):
        w_own(h).wait()
        for j in range(1, N_Y):
            w_over(h, j, 1 - core).wait_recv()
        landed_all(near.at[h, :, :, pl.ds(DH, (N_Y - 1) * DH)], y_recv.at[h])
        near[h, :, :, pl.ds(0, DH)] = attn[:, y_at, :, pl.ds(h * DH, DH)]
        mine = near[h].reshape(2 * rows, N_Y * DH)

        def step(n, carry):
            where = at(n, cols)
            value = jnp.dot(mine, wv[h, :, where], preferred_element_type=jnp.float32)
            if h:
                value = value + total[:, where]
            total[:, where] = value
            if h == heads - 1:
                give[:, where] = total[at(1 - x_at, rows), where].astype(jnp.bfloat16)
                share_out(n).start()
            return carry

        lax.fori_loop(0, n_cols, step, 0)

    def cross_of(h):
        def step(part, carry):
            attend_cross(h, part)
            return carry

        lax.fori_loop(0, 2, step, 0)

    def x_first():
        for j in range(n_head):
            x_out(j).start()

    def x_second():
        landed_all(kvx.at[:, pl.ds(blk, span), :], x_recv.at[0])
        halo_out(0).start()
        halo_out(1).start()

    def x_third():
        halo_out(0).wait_recv()
        halo_out(1).wait_recv()

    for h in range(heads):
        acc[h] = jnp.zeros((span, 2 * DH), jnp.float32)
        peak[h] = jnp.full((span, DH), LOW, jnp.float32)
    pl.semaphore_wait(barrier, len(partners))
    for h in range(heads):
        for j in range(n_head):
            kv_out(h, j).start()
        if h == 0:
            for j in range(n_head):
                q_out(j).start()
    final = heads * (n_phases - 1)
    late = final + 3
    events = [
        (min(3, late), lambda: w_first(0)), (min(4, late), lambda: w_first(1)), (min(5, late), lambda: w_first(2)),
        (min(5, final), x_first), (min(8, late), lambda: w_second(0)),
        (min(9, final), x_second), (min(10, late), lambda: w_second(1)),
        (min(11, final), x_third), (min(11, final), lambda: cross_of(0)),
        (min(12, late), lambda: w_second(2)), (min(12, late), lambda: w_third(0)),
        (min(12, late), lambda: cross_of(1)), (min(14, late), lambda: w_third(1)), (min(14, late), lambda: cross_of(2)),
        (min(16, late), lambda: w_third(2)), (final + 3, lambda: project(0)),
    ]

    def advance(i, carry):
        for when in sorted({event[0] for event in events}):
            @pl.when(i == when)
            def _():
                for event in events:
                    if event[0] == when:
                        event[1]()

        tick, h = i // heads, i % heads
        phase = tick - LAG * h
        for at_phase in range(n_phases):
            @pl.when(phase == at_phase)
            def _():
                pass_on(h, at_phase)

        @pl.when(i == 0)
        def _():
            q_out(0).wait()
            landed_all(q.at[others, :], q_recv.at[0])

        use(i - 1)
        return carry

    def use(i):
        tick, h = i // heads, i % heads
        phase = tick - LAG * h

        @pl.when((i >= 0) & (phase > 0) & (phase < n_phases))
        def _():
            def step(pair, inner):
                @pl.when(pair == 2 * half - 1)
                def _():
                    ring(h, *over("x")).wait_recv()

                attend(h, pair)
                return inner

            lax.fori_loop(2 * phase - 2, 2 * phase, step, 0)

        for at_head in range(heads):
            @pl.when((i >= 0) & (phase == n_phases - 1) & (h == at_head))
            def _():
                lanes = pl.ds(at_head * DH, DH)
                self_out = acc[at_head, :, pl.ds(0, DH)] / acc[at_head, :, pl.ds(DH, DH)]
                value = (self_out + cross[:, lanes]).astype(jnp.bfloat16)
                attn[:, :, :, lanes] = value.reshape(2, N_Y, rows, DH)
                for j in range(1, N_Y):
                    attn_out(at_head, j).start()

    steps = heads * (n_phases + LAG * (heads - 1))
    lax.fori_loop(0, steps, advance, 0)
    use(steps - 1)
    for h in range(1, heads):
        project(h)

    def collect(n, carry):
        where = at(n, cols)
        share_out(n).wait_recv()
        out[:, where] = (total[at(x_at, rows), where] + take[:, where].astype(jnp.float32)).astype(jnp.bfloat16)
        return carry

    lax.fori_loop(0, n_cols, collect, 0)

    landed_all(kv.at[0, :, :, others, :], a_send.at[0])
    landed_all(q.at[others, :], q_send.at[0])
    landed_all(kvx.at[:, pl.ds(0, span), :], x_send.at[0])
    landed_all(kvx.at[:, pl.ds(0, span), :], h_send.at[0])
    landed_all(kv.at[pl.ds(0, len(place) - 1)], g_send.at[0])
    landed_all(wv.at[:, pl.ds(0, (N_Y - 1) * DH), :], w_send.at[0])
    landed_all(near.at[:, :, :, pl.ds(0, (N_Y - 1) * DH)], y_send.at[0])
    landed_all(give, r_send.at[0])


def on_device(mesh_shape, acts, out_weight, pairs):
    n_head, n_seq = mesh_shape["head"], mesh_shape["seq"]
    rows, model = acts.shape[1], acts.shape[3]
    width = out_weight.shape[1]
    heads, span = width // DH, rows * n_head
    cols = math.gcd(model, 512)
    n_cols = model // cols
    n_pos = n_seq
    dma = pltpu.SemaphoreType.DMA
    bf16, f32 = jnp.bfloat16, jnp.float32
    result = pl.pallas_call(
        functools.partial(kernel, (n_head, n_seq, heads, cols)),
        out_shape=jax.ShapeDtypeStruct((rows, model), bf16),
        in_specs=[pl.BlockSpec(memory_space=pl.ANY), pl.BlockSpec(memory_space=pl.ANY),
                  pl.BlockSpec(memory_space=pltpu.SMEM)],
        out_specs=pl.BlockSpec(memory_space=pltpu.VMEM),
        scratch_shapes=[
            pltpu.VMEM((n_pos, heads, 2, span, DH), bf16),
            pltpu.VMEM((span, width), bf16),
            pltpu.VMEM((2, 2 * span, width), bf16),
            pltpu.VMEM((heads, span, 2 * DH), f32),
            pltpu.VMEM((heads, span, DH), f32),
            pltpu.VMEM((span, width), f32),
            pltpu.VMEM((2, N_Y, rows, width), bf16),
            pltpu.VMEM((heads, 2, rows, N_Y * DH), bf16),
            pltpu.VMEM((heads, N_Y * DH, model), bf16),
            pltpu.VMEM((2 * rows, model), f32),
            pltpu.VMEM((rows, model), bf16),
            pltpu.VMEM((rows, model), bf16),
            dma((1,)), dma((heads,)),
            dma((1,)), dma((1,)),
            dma((1,)), dma((1,)),
            dma((1,)), dma((heads, n_pos // 2 - 1, 2)), dma((heads, n_pos // 2)),
            dma((1,)), dma((2,)),
            dma((1,)), dma((heads, 4 + N_Y)),
            dma((1,)), dma((heads,)),
            dma((1,)), dma((n_cols,)),
            dma((2 * heads + 1,)),
        ],
        compiler_params=pltpu.CompilerParams(
            collective_id=0, has_side_effects=True, vmem_limit_bytes=VMEM_BYTES),
        cost_estimate=pl.CostEstimate(flops=10**10, bytes_accessed=2 * 10**7, transcendentals=10**7),
    )(jnp.transpose(acts[0], (1, 0, 2)), out_weight[0].reshape(heads, DH, model), pairs[0])
    return result[None]


def solution(mesh):
    placed = (
        P("tower", ("seq", "head"), None, None),
        P("tower", "head", None),
        P("tower", "seq", None),
    )
    return jax.shard_map(
        functools.partial(on_device, dict(mesh.shape)),
        mesh=mesh,
        in_specs=placed,
        out_specs=P("tower", ("seq", "head"), None),
        check_vma=False,
    )
```

time: 120 us -> 106 us (0.88)
  Pallas kernels: 118 us -> 104 us
    pallas_call x1, Pallas kernels: 118 us -> 104 us  [on_device(): pl.pallas_call(functools.partial(kernel, (n_head, n_seq, heads, cols)), o...]
where the time goes in v3:
time: 106 us; the launch traced here: 105 us
  Pallas kernels  104 us (98%)
  local copies, waits for them, and re-layouts  1.77 us (2%)
    pallas_call x1, Pallas kernels, on_device(): pl.pallas_call(functools.partial(kernel, (n_head, n_seq, heads, cols)), o...  104 us

profile of v3, /device:TPU:1, one launch (start us, length us, event | category | flops | bytes accessed | tf_op | source)
XLA Modules:
  0.0 105.5 jit_solution(4556098515449147360)
XLA Ops:
  0.0 103.7 %shard_map.37 = bf16[64,3072]{1,0:T(8,128)(2,1)} custom-call(bf16[5,64,3072]{2,1,0:T(8,128)(2,1)} %bitcast.8, bf16[3,128,3072]{2,1,0:T(8,128)(2,1)} %bitcast.7, s32[2,3]{1,0:T(2,128)} %bitcast.9), custom_call_target="tpu_custom_call" | custom-call | flops 10000000000 | bytes 20000000 | tf_op jit(solution)/shard_map/pallas_call | solution.py:400
  103.7 1.8 %copy.5 = bf16[1,64,3072]{2,1,0:T(8,128)(2,1)} copy(bf16[1,64,3072]{2,1,0:T(8,128)(2,1)} %bitcast.6) | data formatting | bytes 786432

commit v4 on v3

--- a/solution.py
+++ b/solution.py
@@ -11,7 +11,6 @@
 DH = 128
 SCALE = math.log2(math.e) / math.sqrt(DH)
 LOW = -1e30
-LAG = 1
 PARTS = 2
 N_Y = 4
 MESH = pl.DeviceIdType.MESH
@@ -148,9 +147,16 @@
                 for part in parts:
                     ring(h, "x", "x", ways[way], part).wait_recv()
             ring(h, *over("x")).start()
-        if phase > 0:
-            for name in ["own"] if phase == 1 else [f"l{phase - 1}", f"r{phase - 1}"]:
-                ring(h, *over(name)).wait_recv()
+        if 0 < phase < half:
+            handed_over(h, phase)
+        elif phase == half:
+            @pl.when(h == 0)
+            def _():
+                handed_over(h, phase)
+
+    def handed_over(h, phase):
+        for name in ["own"] if phase == 1 else [f"l{phase - 1}", f"r{phase - 1}"]:
+            ring(h, *over(name)).wait_recv()
 
     def hops():
         result = onward("own") + [over("own"), over("x")]
@@ -164,24 +170,30 @@
     def wide(value, times):
         return jnp.concatenate([value] * times, axis=1)
 
-    def attend(h, pair):
-        both = pl.ds(2 * pair, 2)
-        keys = kv[both, h, 0].reshape(2 * span, DH)
-        values = jnp.concatenate([kv[both, h, 1].reshape(2 * span, DH), ones], axis=1)
-        lanes = at(h, DH)
-        parts = [pl.ds(0, blk), pl.ds(blk, blk)]
-        olds = [peak[h, part] for part in parts]
-        scores = [lax.dot_general(q[part, lanes], keys, (((1,), (1,)), ((), ())),
-                                  preferred_element_type=jnp.float32) for part in parts]
+    def attend(blocks):
+        olds, scores, values = [], [], []
+        for h, pair, part in blocks:
+            both = pl.ds(2 * pair, 2)
+            keys = kv[both, h, 0].reshape(2 * span, DH)
+            values.append(jnp.concatenate([kv[both, h, 1].reshape(2 * span, DH), ones], axis=1))
+            olds.append(peak[h, part])
+            scores.append(lax.dot_general(q[part, at(h, DH)], keys, (((1,), (1,)), ((), ())),
+                                          preferred_element_type=jnp.float32))
         results = []
-        for old, score in zip(olds, scores):
+        for old, score, value in zip(olds, scores, values):
             new = jnp.maximum(old, jnp.max(score, axis=1, keepdims=True))
             weights = jnp.exp2((score - wide(new, 2 * span // DH)) * SCALE).astype(jnp.bfloat16)
-            update = jnp.dot(weights, values, preferred_element_type=jnp.float32)
+            update = jnp.dot(weights, value, preferred_element_type=jnp.float32)
             results.append((new, jnp.exp2((old - new) * SCALE), update))
-        for part, (new, shrink, update) in zip(parts, results):
+        for (h, pair, part), (new, shrink, update) in zip(blocks, results):
             acc[h, part] = acc[h, part] * wide(shrink, 2) + update
             peak[h, part] = new
+
+    halves = [pl.ds(0, blk), pl.ds(blk, blk)]
+
+    def before_last(h):
+        handed_over(h, half)
+        attend([(h, 2 * half - 2, part) for part in halves])
 
     def attend_cross(h, part):
         lanes = at(h, DH)
@@ -242,32 +254,61 @@
         w_on(h, 1).wait_recv()
         w_over(h, 2, core).start()
 
-    def attn_out(h, j):
-        lanes = pl.ds(h * DH, DH)
-        return remote(attn.at[:, (y_at + j) % N_Y, :, lanes], near.at[h, :, :, pl.ds(j * DH, DH)],
-                      y_send.at[0], y_recv.at[h], along_y(j))
+    def attn_out(h, home, j):
+        return remote(attn.at[home, (y_at + j) % N_Y, :, pl.ds(h * DH, DH)], near.at[h, home, :, pl.ds(j * DH, DH)],
+                      y_send.at[0], y_recv.at[h, home], along_y(j))
+
+    def finish(h, home):
+        part, lanes = at(home, blk), pl.ds(h * DH, DH)
+        self_out = acc[h, part, pl.ds(0, DH)] / acc[h, part, pl.ds(DH, DH)]
+        value = (self_out + cross[part, lanes]).astype(jnp.bfloat16)
+        attn[home, :, :, lanes] = value.reshape(N_Y, rows, DH)
+        for j in range(1, N_Y):
+            attn_out(h, home, j).start()
+
+    def gathered(h, home):
+        landed_all(near.at[h, home, :, pl.ds(DH, (N_Y - 1) * DH)], y_recv.at[h, home])
+        near[h, home, :, pl.ds(0, DH)] = attn[home, y_at, :, pl.ds(h * DH, DH)]
+
+    def weights_here(h):
+        w_own(h).wait()
+        for j in range(1, N_Y):
+            w_over(h, j, 1 - core).wait_recv()
 
     def share_out(n):
         return remote(give.at[:, at(n, cols)], take.at[:, at(n, cols)], r_send.at[0], r_recv.at[n],
                       (t, s, (1 - x_at) * N_Y + y_at))
 
-    def project(h):
-        w_own(h).wait()
-        for j in range(1, N_Y):
-            w_over(h, j, 1 - core).wait_recv()
-        landed_all(near.at[h, :, :, pl.ds(DH, (N_Y - 1) * DH)], y_recv.at[h])
-        near[h, :, :, pl.ds(0, DH)] = attn[:, y_at, :, pl.ds(h * DH, DH)]
-        mine = near[h].reshape(2 * rows, N_Y * DH)
+    def project_first():
+        weights_here(0)
+        gathered(0, 0)
+        gathered(0, 1)
+        mine = near[0].reshape(2 * rows, N_Y * DH)
 
         def step(n, carry):
             where = at(n, cols)
-            value = jnp.dot(mine, wv[h, :, where], preferred_element_type=jnp.float32)
-            if h:
-                value = value + total[:, where]
-            total[:, where] = value
-            if h == heads - 1:
-                give[:, where] = total[at(1 - x_at, rows), where].astype(jnp.bfloat16)
+            total[:, where] = jnp.dot(mine, wv[0, :, where], preferred_element_type=jnp.float32)
+            return carry
+
+        lax.fori_loop(0, n_cols, step, 0)
+
+    def project_late(home, send):
+        for h in range(1, heads):
+            if send:
+                weights_here(h)
+            gathered(h, home)
+        mine = [near[h, home] for h in range(1, heads)]
+
+        def step(n, carry):
+            where = at(n, cols)
+            value = total[at(home, rows), where]
+            for h in range(1, heads):
+                value += jnp.dot(mine[h - 1], wv[h, :, where], preferred_element_type=jnp.float32)
+            if send:
+                give[:, where] = value.astype(jnp.bfloat16)
                 share_out(n).start()
+            else:
+                total[at(home, rows), where] = value
             return carry
 
         lax.fori_loop(0, n_cols, step, 0)
@@ -305,13 +346,13 @@
     final = heads * (n_phases - 1)
     late = final + 3
     events = [
-        (min(3, late), lambda: w_first(0)), (min(4, late), lambda: w_first(1)), (min(5, late), lambda: w_first(2)),
-        (min(5, final), x_first), (min(8, late), lambda: w_second(0)),
-        (min(9, final), x_second), (min(10, late), lambda: w_second(1)),
+        (min(5, final), x_first), (min(3, late), lambda: w_first(0)),
+        (min(4, late), lambda: w_first(1)), (min(5, late), lambda: w_first(2)),
+        (min(9, final), x_second), (min(8, late), lambda: w_second(0)),
         (min(11, final), x_third), (min(11, final), lambda: cross_of(0)),
-        (min(12, late), lambda: w_second(2)), (min(12, late), lambda: w_third(0)),
-        (min(12, late), lambda: cross_of(1)), (min(14, late), lambda: w_third(1)), (min(14, late), lambda: cross_of(2)),
-        (min(16, late), lambda: w_third(2)), (final + 3, lambda: project(0)),
+        (min(10, late), lambda: w_second(1)), (min(12, late), lambda: cross_of(1)),
+        (min(13, late), lambda: cross_of(2)), (min(12, late), lambda: w_second(2)),
+        (min(12, late), lambda: w_third(0)), (min(14, late), lambda: w_third(1)), (min(16, late), lambda: w_third(2)),
     ]
 
     def advance(i, carry):
@@ -323,7 +364,7 @@
                         event[1]()
 
         tick, h = i // heads, i % heads
-        phase = tick - LAG * h
+        phase = tick - jnp.where(h == 0, 0, 1)
         for at_phase in range(n_phases):
             @pl.when(phase == at_phase)
             def _():
@@ -339,35 +380,41 @@
 
     def use(i):
         tick, h = i // heads, i % heads
-        phase = tick - LAG * h
-
-        @pl.when((i >= 0) & (phase > 0) & (phase < n_phases))
+        phase = tick - jnp.where(h == 0, 0, 1)
+
+        @pl.when((i >= 0) & (phase > 0) & (phase < jnp.where(h == 0, n_phases, n_phases - 1)))
         def _():
             def step(pair, inner):
                 @pl.when(pair == 2 * half - 1)
                 def _():
                     ring(h, *over("x")).wait_recv()
 
-                attend(h, pair)
+                attend([(h, pair, part) for part in halves])
                 return inner
 
             lax.fori_loop(2 * phase - 2, 2 * phase, step, 0)
 
-        for at_head in range(heads):
-            @pl.when((i >= 0) & (phase == n_phases - 1) & (h == at_head))
-            def _():
-                lanes = pl.ds(at_head * DH, DH)
-                self_out = acc[at_head, :, pl.ds(0, DH)] / acc[at_head, :, pl.ds(DH, DH)]
-                value = (self_out + cross[:, lanes]).astype(jnp.bfloat16)
-                attn[:, :, :, lanes] = value.reshape(2, N_Y, rows, DH)
-                for j in range(1, N_Y):
-                    attn_out(at_head, j).start()
-
-    steps = heads * (n_phases + LAG * (heads - 1))
+        @pl.when((i >= 0) & (phase == n_phases - 1) & (h == 0))
+        def _():
+            finish(0, 0)
+            finish(0, 1)
+
+    steps = heads * (n_phases + 1)
     lax.fori_loop(0, steps, advance, 0)
     use(steps - 1)
-    for h in range(1, heads):
-        project(h)
+
+    late_heads = range(1, heads)
+    for h in late_heads:
+        before_last(h)
+    for h in late_heads:
+        ring(h, *over("x")).wait_recv()
+    for home in (1 - x_at, x_at):
+        attend([(h, 2 * half - 1, at(home, blk)) for h in late_heads])
+        for h in late_heads:
+            finish(h, home)
+    project_first()
+    project_late(1 - x_at, True)
+    project_late(x_at, False)
 
     def collect(n, carry):
         where = at(n, cols)
@@ -422,7 +469,7 @@
             dma((1,)), dma((heads, n_pos // 2 - 1, 2)), dma((heads, n_pos // 2)),
             dma((1,)), dma((2,)),
             dma((1,)), dma((heads, 4 + N_Y)),
-            dma((1,)), dma((heads,)),
+            dma((1,)), dma((heads, 2)),
             dma((1,)), dma((n_cols,)),
             dma((2 * heads + 1,)),
         ],

time: 106 us -> 102 us (0.962)
  Pallas kernels: 104 us -> 100 us
    pallas_call x1, Pallas kernels: 104 us -> 100 us  [on_device(): pl.pallas_call(functools.partial(kernel, (n_head, n_seq, heads, cols)), o...]
where the time goes in v4:
time: 102 us
  Pallas kernels  100 us (98%)
  local copies, waits for them, and re-layouts  1.77 us (2%)
    pallas_call x1, Pallas kernels, on_device(): pl.pallas_call(functools.partial(kernel, (n_head, n_seq, heads, cols)), o...  100 us

profile of v4, /device:TPU:1, one launch (start us, length us, event | category | flops | bytes accessed | tf_op | source)
XLA Modules:
  0.0 102.1 jit_solution(255044140574855789)
XLA Ops:
  0.0 100.3 %shard_map.37 = bf16[64,3072]{1,0:T(8,128)(2,1)} custom-call(bf16[5,64,3072]{2,1,0:T(8,128)(2,1)} %bitcast.8, bf16[3,128,3072]{2,1,0:T(8,128)(2,1)} %bitcast.7, s32[2,3]{1,0:T(2,128)} %bitcast.9), custom_call_target="tpu_custom_call" | custom-call | flops 10000000000 | bytes 20000000 | tf_op jit(solution)/shard_map/pallas_call | solution.py:447
  100.3 1.8 %copy.5 = bf16[1,64,3072]{2,1,0:T(8,128)(2,1)} copy(bf16[1,64,3072]{2,1,0:T(8,128)(2,1)} %bitcast.6) | data formatting | bytes 786432

commit v5 on v4

--- a/solution.py
+++ b/solution.py
@@ -24,9 +24,9 @@
     return {name: i for i, name in enumerate(names + ["x", "sx"])}
 
 
-def kernel(sizes, acts, weight, pairs, out, kv, q, kvx, acc, peak, cross, attn, near, wv, total, give, take,
+def kernel(sizes, acts, weight, pairs, out, kv, q, kvx, acc, peak, cross, attn, near, wv, total, give, take, done,
            a_send, a_recv, q_send, q_recv, x_send, x_recv, g_send, g_recv, o_recv, h_send, h_recv,
-           w_send, w_recv, y_send, y_recv, r_send, r_recv, l_sem):
+           w_send, w_recv, y_send, y_recv, r_send, r_recv, l_sem, d_sem):
     n_head, n_seq, heads, cols = sizes
     rows = acts.shape[1]
     span = rows * n_head
@@ -51,9 +51,9 @@
     def head_of(j):
         return (me + j) % n_head
 
-    partners = [(t, s, head_of(j)) for j in range(1, n_head)]
+    partners = [(t, up, me), (t, down, me), (t, far, me), (t, sib, me)]
+    partners += [(t, s, head_of(j)) for j in range(1, n_head)]
     partners += [(1 - t, s, head_of(j)) for j in range(n_head)]
-    partners += [(t, up, me), (t, down, me), (t, sib, me), (t, far, me)]
     barrier = pltpu.get_barrier_semaphore()
     for device in partners:
         pl.semaphore_signal(barrier, inc=1, device_id=device, device_id_type=MESH)
@@ -96,7 +96,7 @@
     def ring(h, source, target, device, part=None):
         rows_of = pl.ds(0, span) if part is None else pl.ds(part * blk, blk)
         if target[0] == "s":
-            landed = o_recv.at[h, stops.index(target[1:])]
+            landed = o_recv.at[h, stops.index(target[1:]) + (part or 0)]
         else:
             landed = g_recv.at[h, stops.index(target) - 1, 0 if part is None else part]
         return remote(kv.at[place[source], h, :, rows_of, :], kv.at[place[target], h, :, rows_of, :],
@@ -128,8 +128,10 @@
         if phase == 0:
             kv_out(h, 0).wait()
             landed_all(kv.at[place["own"], h, :, others, :], a_recv.at[h])
-            for hop in onward("own"):
-                ring(h, *hop).start()
+            left, right = [[hop for hop in onward("own") if hop[2] is ways[way]] for way in "lr"]
+            for pair in zip(left, right[::-1]):
+                for hop in pair:
+                    ring(h, *hop).start()
             ring(h, *over("own")).start()
         elif phase < half:
             for k in range(PARTS):
@@ -146,7 +148,7 @@
             for way, parts in parts_of(half).items():
                 for part in parts:
                     ring(h, "x", "x", ways[way], part).wait_recv()
-            ring(h, *over("x")).start()
+                    ring(h, *over("x"), part).start()
         if 0 < phase < half:
             handed_over(h, phase)
         elif phase == half:
@@ -349,9 +351,9 @@
         (min(5, final), x_first), (min(3, late), lambda: w_first(0)),
         (min(4, late), lambda: w_first(1)), (min(5, late), lambda: w_first(2)),
         (min(9, final), x_second), (min(8, late), lambda: w_second(0)),
-        (min(11, final), x_third), (min(11, final), lambda: cross_of(0)),
-        (min(10, late), lambda: w_second(1)), (min(12, late), lambda: cross_of(1)),
-        (min(13, late), lambda: cross_of(2)), (min(12, late), lambda: w_second(2)),
+        (min(12, final), x_third), (min(12, final), lambda: cross_of(0)),
+        (min(10, late), lambda: w_second(1)), (min(13, late), lambda: cross_of(1)),
+        (min(14, late), lambda: cross_of(2)), (min(12, late), lambda: w_second(2)),
         (min(12, late), lambda: w_third(0)), (min(14, late), lambda: w_third(1)), (min(16, late), lambda: w_third(2)),
     ]
 
@@ -387,7 +389,8 @@
             def step(pair, inner):
                 @pl.when(pair == 2 * half - 1)
                 def _():
-                    ring(h, *over("x")).wait_recv()
+                    for part in range(2):
+                        ring(h, *over("x"), part).wait_recv()
 
                 attend([(h, pair, part) for part in halves])
                 return inner
@@ -407,7 +410,8 @@
     for h in late_heads:
         before_last(h)
     for h in late_heads:
-        ring(h, *over("x")).wait_recv()
+        for part in range(2):
+            ring(h, *over("x"), part).wait_recv()
     for home in (1 - x_at, x_at):
         attend([(h, 2 * half - 1, at(home, blk)) for h in late_heads])
         for h in late_heads:
@@ -419,10 +423,13 @@
     def collect(n, carry):
         where = at(n, cols)
         share_out(n).wait_recv()
-        out[:, where] = (total[at(x_at, rows), where] + take[:, where].astype(jnp.float32)).astype(jnp.bfloat16)
+        done[:, where] = (total[at(x_at, rows), where] + take[:, where].astype(jnp.float32)).astype(jnp.bfloat16)
+        pltpu.make_async_copy(done.at[:, where], out.at[:, where], d_sem.at[0]).start()
         return carry
 
     lax.fori_loop(0, n_cols, collect, 0)
+
+    landed_all(done, d_sem.at[0])
 
     landed_all(kv.at[0, :, :, others, :], a_send.at[0])
     landed_all(q.at[others, :], q_send.at[0])
@@ -449,7 +456,7 @@
         out_shape=jax.ShapeDtypeStruct((rows, model), bf16),
         in_specs=[pl.BlockSpec(memory_space=pl.ANY), pl.BlockSpec(memory_space=pl.ANY),
                   pl.BlockSpec(memory_space=pltpu.SMEM)],
-        out_specs=pl.BlockSpec(memory_space=pltpu.VMEM),
+        out_specs=pl.BlockSpec(memory_space=pl.ANY),
         scratch_shapes=[
             pltpu.VMEM((n_pos, heads, 2, span, DH), bf16),
             pltpu.VMEM((span, width), bf16),
@@ -463,15 +470,16 @@
             pltpu.VMEM((2 * rows, model), f32),
             pltpu.VMEM((rows, model), bf16),
             pltpu.VMEM((rows, model), bf16),
+            pltpu.VMEM((rows, model), bf16),
             dma((1,)), dma((heads,)),
             dma((1,)), dma((1,)),
             dma((1,)), dma((1,)),
-            dma((1,)), dma((heads, n_pos // 2 - 1, 2)), dma((heads, n_pos // 2)),
+            dma((1,)), dma((heads, n_pos // 2 - 1, 2)), dma((heads, n_pos // 2 + 1)),
             dma((1,)), dma((2,)),
             dma((1,)), dma((heads, 4 + N_Y)),
             dma((1,)), dma((heads, 2)),
             dma((1,)), dma((n_cols,)),
-            dma((2 * heads + 1,)),
+            dma((2 * heads + 1,)), dma((1,)),
         ],
         compiler_params=pltpu.CompilerParams(
             collective_id=0, has_side_effects=True, vmem_limit_bytes=VMEM_BYTES),

time: 102 us -> 102 us (level)
  no operation moved by 1% of the time
where the time goes in v5:
time: 102 us
  Pallas kernels  100 us (98%)
  local copies, waits for them, and re-layouts  1.77 us (2%)
    pallas_call x1, Pallas kernels, on_device(): pl.pallas_call(functools.partial(kernel, (n_head, n_seq, heads, cols)), o...  100 us

profile of v5, /device:TPU:1, one launch (start us, length us, event | category | flops | bytes accessed | tf_op | source)
XLA Modules:
  0.0 102.0 jit_solution(4774765305499361017)
XLA Ops:
  0.0 100.2 %shard_map.37 = bf16[64,3072]{1,0:T(8,128)(2,1)} custom-call(bf16[5,64,3072]{2,1,0:T(8,128)(2,1)} %bitcast.8, bf16[3,128,3072]{2,1,0:T(8,128)(2,1)} %bitcast.7, s32[2,3]{1,0:T(2,128)} %bitcast.9), custom_call_target="tpu_custom_call" | custom-call | flops 10000000000 | bytes 20000000 | tf_op jit(solution)/shard_map/pallas_call | solution.py:454
  100.3 1.8 %copy.5 = bf16[1,64,3072]{2,1,0:T(8,128)(2,1)} copy(bf16[1,64,3072]{2,1,0:T(8,128)(2,1)} %bitcast.6) | data formatting | bytes 786432

commit v6 on v5

--- a/solution.py
+++ b/solution.py
@@ -340,7 +340,7 @@
         peak[h] = jnp.full((span, DH), LOW, jnp.float32)
     pl.semaphore_wait(barrier, len(partners))
     for h in range(heads):
-        for j in range(n_head):
+        for j in sorted(range(n_head), key=lambda j: -min(j % N_Y, N_Y - j % N_Y)):
             kv_out(h, j).start()
         if h == 0:
             for j in range(n_head):

time: 102 us -> 102 us (level)
  no operation moved by 1% of the time
where the time goes in v6:
time: 102 us
  Pallas kernels  100 us (98%)
  local copies, waits for them, and re-layouts  1.77 us (2%)
    pallas_call x1, Pallas kernels, on_device(): pl.pallas_call(functools.partial(kernel, (n_head, n_seq, heads, cols)), o...  100 us

profile of v6, /device:TPU:1, one launch (start us, length us, event | category | flops | bytes accessed | tf_op | source)
XLA Modules:
  0.0 101.8 jit_solution(9976484730067461022)
XLA Ops:
  0.0 100.0 %shard_map.37 = bf16[64,3072]{1,0:T(8,128)(2,1)} custom-call(bf16[5,64,3072]{2,1,0:T(8,128)(2,1)} %bitcast.8, bf16[3,128,3072]{2,1,0:T(8,128)(2,1)} %bitcast.7, s32[2,3]{1,0:T(2,128)} %bitcast.9), custom_call_target="tpu_custom_call" | custom-call | flops 10000000000 | bytes 20000000 | tf_op jit(solution)/shard_map/pallas_call | solution.py:454
  100.0 1.8 %copy.5 = bf16[1,64,3072]{2,1,0:T(8,128)(2,1)} copy(bf16[1,64,3072]{2,1,0:T(8,128)(2,1)} %bitcast.6) | data formatting | bytes 786432
